TPU v7x, 32 devices: a whole 2x2x4 slice. The times are simulated.
32 devices in a mesh: blk: 8 (over y, x, core), uly: 4 (over z).
Axes of the slice: x: 2, y: 2, z: 4, core: 2. Of those that a mesh axis runs over, the one named last changes fastest.
Arguments:
- hidden_in: bfloat16 [2048, 3072], P(('blk', 'uly')), may hold values from -6 to 6
- cached_out: bfloat16 [2048, 3072], P(('blk', 'uly')), may hold values from -6 to 6
- cache_keys: bfloat16 [2048, 3072], P(('blk', 'uly')), may hold values from -288 to 288
- cache_values: bfloat16 [2048, 3072], P(('blk', 'uly')), may hold values from -36 to 36
- refresh_idx: int32 [512], P(('blk', 'uly')), may hold values from -1 to 63, as said below
- modulation: float32 [6, 3072], replicated, may hold values from -3 to 3
- q_gain: float32 [128], replicated, may hold values from 1.5 to 4
- w_query: bfloat16 [3072, 3072], P(None, 'uly'), may hold values from -0.109375 to 0.109375
- w_out: bfloat16 [3072, 3072], P('uly'), may hold values from -0.109375 to 0.109375
- w_up: bfloat16 [3072, 12288], P(None, 'blk'), may hold values from -0.109375 to 0.109375
- w_down: bfloat16 [12288, 3072], P('blk'), may hold values from -0.0546875 to 0.0546875
Outputs:
- features: bfloat16 [2048, 3072], P(('blk', 'uly'))
Inputs may be any that keep to these rules, and one draw needn't show every extreme that they name: `refresh_idx`: each device's 16 slots name distinct positions among that device's own 64 positions, live slots first and -1 in the rest. Among the devices that share a blk index, one has all 16 slots live and every other at most 8; so such a group has at most 40 live slots, and some group has exactly 40.
All inputs are finite; a program needn't handle non-finite values.
Results may differ from a plain program's by a relative error of at most 0.023.
The roundings to bfloat16 on the way count: a program that leaves them out, or rounds other values in their place, can miss the bound.
Values may be sent and summed in bfloat16 or wider, within the bound.
No kernel may reach another device: no remote copies, remote signals or barrier semaphores. Data moves between devices by JAX's collectives and lax.ppermute only.
A program may use at most 128 MiB of HBM per device.

v0:
```python
import math

import jax
import jax.numpy as jnp
from jax import lax
from jax.sharding import PartitionSpec as P

DH = 128


def layer_norm(row_block, shift_by, scale_by):
    average = jnp.mean(row_block, axis=-1, keepdims=True)
    centred = row_block - average
    spread = jnp.mean(centred * centred, axis=-1, keepdims=True)
    return centred * lax.rsqrt(spread + 1e-06) * (1.0 + scale_by) + shift_by


def row_peak(local_max):
    return lax.pmax(local_max, "blk")


def block_scores(query_block, key_rows):
    return jnp.einsum("qhd,khd->hqk", query_block, key_rows, preferred_element_type=jnp.float32)


def block_finish(scores, maxima, value_rows):
    weights = jnp.exp(scores - maxima[..., None])
    denominators = jnp.sum(weights, axis=-1)
    weighted = jnp.einsum(
        "hqk,khd->qhd", weights.astype(jnp.bfloat16), value_rows, preferred_element_type=jnp.float32
    )
    return (weighted, denominators)


def body(
    hidden_in,
    cached_out,
    cache_keys,
    cache_values,
    refresh_idx,
    modulation,
    q_gain,
    w_query,
    w_out,
    w_up,
    w_down,
):
    tokens = hidden_in.shape[0]
    uly_size = lax.axis_size("uly")
    local_heads = w_query.shape[1] // DH
    positions = lax.iota(jnp.int32, tokens)
    select = (positions[:, None] == refresh_idx[None, :]).astype(jnp.bfloat16)
    rows_in = jnp.einsum("ps,pd->sd", select, hidden_in, preferred_element_type=jnp.float32)
    norm_attn = layer_norm(rows_in, modulation[0], modulation[1]).astype(jnp.bfloat16)
    key_split = cache_keys.reshape(tokens, uly_size, local_heads, DH)
    value_split = cache_values.reshape(tokens, uly_size, local_heads, DH)
    key_moved, value_moved = (
        lax.all_to_all(key_split, "uly", split_axis=1, concat_axis=0, tiled=True),
        lax.all_to_all(value_split, "uly", split_axis=1, concat_axis=0, tiled=True),
    )
    key_rows = key_moved[:, 0]
    value_rows = value_moved[:, 0]
    group_rows, group_idx = (
        lax.all_gather(norm_attn, "uly", axis=0, tiled=True),
        lax.all_gather(refresh_idx, "uly", axis=0, tiled=True),
    )
    projected = jnp.dot(group_rows, w_query, preferred_element_type=jnp.float32).reshape(
        -1, local_heads, DH
    )
    squares = jnp.mean(projected * projected, axis=-1, keepdims=True)
    projected = projected * lax.rsqrt(squares + 1e-06) * (q_gain / math.sqrt(DH))
    queries = lax.all_gather(projected.astype(jnp.bfloat16), "blk", axis=0, tiled=True)
    query_count = queries.shape[0]
    block_rows = math.gcd(query_count, 512)
    query_blocks = queries.reshape(query_count // block_rows, block_rows, local_heads, DH)

    def score_only(query_block):
        return block_scores(query_block, key_rows)

    all_scores = lax.map(score_only, query_blocks)
    maxima = row_peak(jnp.max(all_scores, axis=-1))

    def finish_stored(inputs):
        return block_finish(inputs[0], inputs[1], value_rows)

    weighted, denominators = lax.map(finish_stored, (all_scores, maxima))
    weighted = weighted.reshape(query_count, local_heads, DH)
    denominators = jnp.transpose(denominators, (0, 2, 1)).reshape(query_count, local_heads)
    weighted, denominators = (
        lax.psum_scatter(weighted, "blk", scatter_dimension=0, tiled=True),
        lax.psum_scatter(denominators, "blk", scatter_dimension=0, tiled=True),
    )
    attended = (
        (weighted / denominators[..., None]).astype(jnp.bfloat16).reshape(-1, local_heads * DH)
    )
    row_piece = attended
    branch = lax.psum_scatter(
        jnp.dot(row_piece, w_out, preferred_element_type=jnp.float32),
        "uly",
        scatter_dimension=0,
        tiled=True,
    )
    after_attn = rows_in + modulation[2] * branch
    norm_mlp = layer_norm(after_attn, modulation[3], modulation[4]).astype(jnp.bfloat16)
    lifted = jnp.dot(
        lax.all_gather(norm_mlp, "blk", axis=0, tiled=True),
        w_up,
        preferred_element_type=jnp.float32,
    )
    activations = jax.nn.gelu(lifted, approximate=True).astype(jnp.bfloat16)
    row_piece = activations
    mlp_out = lax.psum_scatter(
        jnp.dot(row_piece, w_down, preferred_element_type=jnp.float32).astype(jnp.bfloat16),
        "blk",
        scatter_dimension=0,
        tiled=True,
    ).astype(jnp.float32)
    renewed = (after_attn + modulation[5] * mlp_out).astype(jnp.bfloat16)
    covered = jnp.sum(select.astype(jnp.float32), axis=1, keepdims=True)
    placed = jnp.dot(select, renewed, preferred_element_type=jnp.float32)
    blended = cached_out.astype(jnp.float32) * (1.0 - covered) + placed
    return blended.astype(jnp.bfloat16)


def solution(mesh):
    return jax.shard_map(
        body,
        mesh=mesh,
        in_specs=(
            P(("blk", "uly"), None),
            P(("blk", "uly"), None),
            P(("blk", "uly"), None),
            P(("blk", "uly"), None),
            P(("blk", "uly")),
            P(),
            P(),
            P(None, "uly"),
            P("uly", None),
            P(None, "blk"),
            P("blk", None),
        ),
        out_specs=P(("blk", "uly"), None),
        check_vma=False,
    )
```

profile of v0, /device:TPU:0, one launch (start us, length us, event | category | flops | bytes accessed | tf_op | source)
XLA Modules:
  0.0 254.6 jit_solution(16457897710319390292)
XLA Ops:
  6.5 1.5 reshape.68
  8.1 0.9 copy.41
  9.0 6.3 %all-to-all-start.1 = ((bf16[64,4,6,128]{3,0,2,1:T(8,128)(2,1)}), bf16[64,4,6,128]{3,0,2,1:T(8,128)(2,1)S(1)}, u32[]{:S(2)}, u32[]{:S(2)}) async-start(bf16[64,4,6,128]{3,0,2,1:T(8,128)(2,1)} %copy.41), calls=%async_computation.1 | async-start | bytes 786432 | tf_op jit(solution)/shard_map/all_to_all | solution.py:59
  15.3 2.0 fusion.38
  17.3 1.0 fusion.39
  19.1 16.8 %all_gather.9 = bf16[64,3072]{1,0:T(8,128)(2,1)S(1)} all-gather(bf16[16,3072]{1,0:T(8,128)(2,1)S(1)} %add_convert_fusion.2), channel_id=1, replica_groups=mesh['blk'=8,'uly'=4] {'uly'}, dimensions={0}, use_global_device_ids=true | all-gather | bytes 491520 | tf_op jit(solution)/shard_map/all_gather | solution.py:64
  35.9 3.2 %fusion.43 = f32[64,768]{1,0:T(8,128)S(1)} fusion(bf16[64,3072]{1,0:T(8,128)(2,1)S(1)} %all_gather.9, bf16[3072,768]{1,0:T(8,128)(2,1)} %param.18), kind=kOutput, calls=%fused_computation.62 | convolution fusion | flops 301989888 | bytes 5308416 | tf_op jit(solution)/shard_map/dot_general | solution.py:67
  39.9 0.9 copy.39
  40.8 4.0 %all-to-all-start = ((bf16[64,4,6,128]{3,0,2,1:T(8,128)(2,1)}), bf16[64,4,6,128]{3,0,2,1:T(8,128)(2,1)S(1)}, u32[]{:S(2)}, u32[]{:S(2)}) async-start(bf16[64,4,6,128]{3,0,2,1:T(8,128)(2,1)} %copy.39), calls=%async_computation | async-start | bytes 786432 | tf_op jit(solution)/shard_map/all_to_all | solution.py:58
  44.9 11.5 %all_gather.10 = bf16[512,6,128]{2,0,1:T(8,128)(2,1)} all-gather(bf16[64,6,128]{2,0,1:T(8,128)(2,1)S(1)} %fusion.23), channel_id=1, replica_groups=mesh['blk'=8,'uly'=4] {'blk'}, dimensions={0}, use_global_device_ids=true | all-gather | bytes 884736 | tf_op jit(solution)/shard_map/all_gather | solution.py:72
  57.2 2.3 fusion.40
  59.6 23.6 %pmax.7 = f32[6,512]{1,0:T(8,128)S(1)} all-reduce(f32[6,512]{1,0:T(8,128)} %get-tuple-element.45), channel_id=1, replica_groups=mesh['blk'=8,'uly'=4] {'blk'}, use_global_device_ids=true, to_apply=%region_5.6 | all-reduce | flops 3072 | bytes 24576 | tf_op jit(solution)/shard_map/pmax | solution.py:19
  83.2 1.0 fusion.1
  84.2 1.6 copy.46
  85.8 2.9 %fusion.6 = f32[512,6,128]{2,0,1:T(8,128)} fusion(bf16[256,6,128]{2,0,1:T(8,128)(2,1)} %bitcast.49, f32[6,512,256]{1,2,0:T(8,128)S(1)} %get-tuple-element.46, f32[6,512]{1,0:T(8,128)S(1)} %pmax.7), kind=kOutput, calls=%fused_computation.8 | convolution fusion | flops 202899456 | bytes 5124096 | tf_op jit(solution)/shard_map/while/body/eval_jaxpr/hqk,khd->qhd/dot_general | solution.py:29
  88.8 31.8 %reduce-scatter.13.cloned.1.call-done = f32[64,6]{1,0:T(8,128)} async-done(((f32[512,6]{1,0:T(8,128)}), f32[64,6]{1,0:T(8,128)}) %reduce-scatter.13.cloned.1.call-update) | async-done | bytes 1552
  121.4 41.3 %reduce-scatter.7.cloned.1.call-done = f32[64,6,128]{2,0,1:T(8,128)} async-done(((f32[512,6,128]{2,0,1:T(8,128)}), f32[64,6,128]{2,0,1:T(8,128)}) %reduce-scatter.7.cloned.1.call-update) | async-done | bytes 196624 | tf_op jit(solution)/shard_map/reduce_scatter | solution.py:90
  162.8 4.3 %fusion.24 = f32[64,3072]{1,0:T(8,128)} fusion(bf16[768,3072]{1,0:T(8,128)(2,1)} %param.19, f32[64,6,128]{2,0,1:T(8,128)} %reduce-scatter.7.cloned.1.call-done, f32[64,6]{0,1:T(8,128)S(1)} %copy.47), kind=kOutput, calls=%fused_computation.33 | convolution fusion | flops 302088192 | bytes 5703168 | tf_op jit(solution)/shard_map/dot_general | solution.py:98
  167.2 23.4 %reduce-scatter.9.cloned.1.call-done = f32[16,3072]{1,0:T(8,128)} async-done(((f32[64,3072]{1,0:T(8,128)}), f32[16,3072]{1,0:T(8,128)}) %reduce-scatter.9.cloned.1.call-update) | async-done | bytes 196624 | tf_op jit(solution)/shard_map/reduce_scatter | solution.py:97
  190.5 1.1 fusion.37
  192.0 10.4 %all_gather.11 = bf16[128,3072]{1,0:T(8,128)(2,1)S(1)} all-gather(bf16[16,3072]{1,0:T(8,128)(2,1)S(1)} %add_convert_fusion.1), channel_id=1, replica_groups=mesh['blk'=8,'uly'=4] {'blk'}, dimensions={0}, use_global_device_ids=true | all-gather | bytes 884736 | tf_op jit(solution)/shard_map/all_gather | solution.py:106
  202.3 10.2 %convolution_convert_fusion = bf16[128,3072]{1,0:T(8,128)(2,1)} fusion(bf16[1536,3072]{1,0:T(8,128)(2,1)} %param.21, bf16[128,3072]{1,0:T(8,128)(2,1)S(1)} %all_gather.11, bf16[3072,1536]{1,0:T(8,128)(2,1)} %param.20), kind=kOutput, calls=%fused_computation | convolution fusion | flops 2418081792 | bytes 20447232 | tf_op jit(solution)/shard_map/dot_general | solution.py:113
  212.7 33.4 %reduce-scatter.11.cloned.1.call-done = bf16[16,3072]{1,0:T(8,128)(2,1)} async-done(((bf16[128,3072]{1,0:T(8,128)(2,1)}), bf16[16,3072]{1,0:T(8,128)(2,1)}) %reduce-scatter.11.cloned.1.call-update) | async-done | bytes 98320 | tf_op jit(solution)/shard_map/reduce_scatter | solution.py:112
  246.1 2.0 fusion
  (52 shorter events, 3.9 us)
Async XLA Ops:
  6.5 10.8 %copy-start = (bf16[64,3072]{1,0:T(8,128)(2,1)S(1)}, bf16[64,3072]{1,0:T(8,128)(2,1)}, u32[]{:S(2)}) copy-start(bf16[64,3072]{1,0:T(8,128)(2,1)} %param.11) | copy-start | bytes 1179652
  8.1 31.3 %copy-start.3 = (bf16[64,3072]{1,0:T(8,128)(2,1)S(1)}, bf16[64,3072]{1,0:T(8,128)(2,1)}, u32[]{:S(2)}) copy-start(bf16[64,3072]{1,0:T(8,128)(2,1)} %param.13) | copy-start | bytes 1179652
  9.0 31.8 %all-to-all-start.1 = ((bf16[64,4,6,128]{3,0,2,1:T(8,128)(2,1)}), bf16[64,4,6,128]{3,0,2,1:T(8,128)(2,1)S(1)}, u32[]{:S(2)}, u32[]{:S(2)}) async-start(bf16[64,4,6,128]{3,0,2,1:T(8,128)(2,1)} %copy.41), calls=%async_computation.1 | async-start | bytes 786432 | tf_op jit(solution)/shard_map/all_to_all | solution.py:59
  18.3 0.7 copy-start.1
  19.0 25.8 %copy-start.10 = (f32[128]{0:T(128)S(1)}, f32[128]{0:T(128)}, u32[]{:S(2)}) copy-start(f32[128]{0:T(128)} %param.17) | copy-start | bytes 1540
  40.8 16.4 %all-to-all-start = ((bf16[64,4,6,128]{3,0,2,1:T(8,128)(2,1)}), bf16[64,4,6,128]{3,0,2,1:T(8,128)(2,1)S(1)}, u32[]{:S(2)}, u32[]{:S(2)}) async-start(bf16[64,4,6,128]{3,0,2,1:T(8,128)(2,1)} %copy.39), calls=%async_computation | async-start | bytes 786432 | tf_op jit(solution)/shard_map/all_to_all | solution.py:58
  44.8 75.8 %reduce-scatter.13.cloned.1.call-start = ((), (), s32[]{:S(2)}) async-start(), calls=%async_computation.9 | async-start | bytes 294912
  85.8 77.0 %reduce-scatter.7.cloned.1.call-start = ((), (), s32[]{:S(2)}) async-start(), calls=%async_computation.6 | async-start | bytes 1769472 | tf_op jit(solution)/shard_map/reduce_scatter | solution.py:90
  88.7 101.8 %copy-start.2 = (f32[16,3072]{1,0:T(8,128)S(1)}, f32[16,3072]{1,0:T(8,128)}, u32[]{:S(2)}) copy-start(f32[16,3072]{1,0:T(8,128)} %copy-done.1) | copy-start | bytes 589828
  88.7 101.8 %copy-start.8 = (f32[1,3072]{1,0:T(1,128)S(1)}, f32[1,3072]{1,0:T(1,128)}, u32[]{:S(2)}) copy-start(f32[1,3072]{1,0:T(1,128)} %get-tuple-element.32) | copy-start | bytes 36868
  88.7 103.1 %copy-start.6 = (f32[1,3072]{1,0:T(1,128)S(1)}, f32[1,3072]{1,0:T(1,128)}, u32[]{:S(2)}) copy-start(f32[1,3072]{1,0:T(1,128)} %get-tuple-element.33) | copy-start | bytes 36868
  88.7 103.1 %copy-start.7 = (f32[1,3072]{1,0:T(1,128)S(1)}, f32[1,3072]{1,0:T(1,128)}, u32[]{:S(2)}) copy-start(f32[1,3072]{1,0:T(1,128)} %get-tuple-element.40) | copy-start | bytes 36868
  88.8 101.8 %reduce-scatter.9.cloned.1.call-start = ((), (), s32[]{:S(2)}) async-start(), calls=%async_computation.7 | async-start | bytes 983040 | tf_op jit(solution)/shard_map/reduce_scatter | solution.py:97
  167.1 79.0 %reduce-scatter.11.cloned.1.call-start = ((), (), s32[]{:S(2)}) async-start(), calls=%async_computation.8 | async-start | bytes 884736 | tf_op jit(solution)/shard_map/reduce_scatter | solution.py:112
  202.3 10.2 %copy-start.9 = (s32[16]{0:T(128)S(1)}, s32[16]{0:T(128)}, u32[]{:S(2)}) copy-start(s32[16]{0:T(128)} %param.15) | copy-start | bytes 196
  202.3 43.7 %copy-start.4 = (bf16[64,3072]{1,0:T(8,128)(2,1)S(1)}, bf16[64,3072]{1,0:T(8,128)(2,1)}, u32[]{:S(2)}) copy-start(bf16[64,3072]{1,0:T(8,128)(2,1)} %param.12) | copy-start | bytes 1179652
  202.3 43.7 %copy-start.5 = (f32[1,3072]{1,0:T(1,128)S(1)}, f32[1,3072]{1,0:T(1,128)}, u32[]{:S(2)}) copy-start(f32[1,3072]{1,0:T(1,128)} %get-tuple-element.29) | copy-start | bytes 36868
Sparse Core Ops, SparseCore 0:
  85.9 34.6 reduce-scatter.12
  124.3 38.4 reduce-scatter.6
  167.2 23.2 reduce-scatter.8
  212.7 33.3 reduce-scatter.10
where the time goes:
time: 255 us
  waiting for transfers between devices  130 us (51%)
  blocking collectives  62.3 us (24%)
  matrix products  25.9 us (10%)
  between operations  13.3 us (5%)
  starting transfers between devices  10.4 us (4%)
  local copies, waits for them, and re-layouts  7.62 us (3%)
  other arithmetic  5.11 us (2%)
    reduce_scatter x1, waiting for transfers between devices, body(): lax.psum_scatter(weighted, 'blk', scatter_dimension=0, tiled=True)  41.3 us
    reduce_scatter x1, waiting for transfers between devices, body(): lax.psum_scatter(jnp.dot(row_piece, w_down, preferred_element_type=jnp.fl...  33.4 us
    unnamed x5, waiting for transfers between devices  31.9 us
    pmax x1, blocking collectives, row_peak(): return lax.pmax(local_max, 'blk')  23.6 us
    reduce_scatter x1, waiting for transfers between devices, body(): lax.psum_scatter(jnp.dot(row_piece, w_out, preferred_element_type=jnp.flo...  23.4 us
    all_gather x1, blocking collectives, body(): lax.all_gather(norm_attn, 'uly', axis=0, tiled=True)  16.8 us
    all_gather x1, blocking collectives, body(): lax.all_gather(projected.astype(jnp.bfloat16), 'blk', axis=0, tiled=True)  11.5 us
    all_gather x1, blocking collectives, body(): lax.all_gather(norm_mlp, 'blk', axis=0, tiled=True)  10.4 us
  transfers between devices with their start and end apart: 6, of which 4 were waited for; matrix products, arithmetic and copies ran while one was open for 5% of the time, Pallas kernels for 0%

commit v1 on v0

v1 whole, which is shorter than its diff:
```python
import math

import jax
import jax.numpy as jnp
from jax import lax
from jax.sharding import PartitionSpec as P

DH = 128
OTHER = 8


def layer_norm(row_block, shift_by, scale_by):
    average = jnp.mean(row_block, axis=-1, keepdims=True)
    centred = row_block - average
    spread = jnp.mean(centred * centred, axis=-1, keepdims=True)
    return centred * lax.rsqrt(spread + 1e-06) * (1.0 + scale_by) + shift_by


def swap(parts, axis):
    return lax.all_to_all(parts, axis, split_axis=0, concat_axis=0, tiled=True)


def gather_permute(rows, axis):
    size = lax.axis_size(axis)
    me = lax.axis_index(axis)
    pieces = [rows]
    for step in range(1, size):
        pieces.append(lax.ppermute(rows, axis, [(i, (i + step) % size) for i in range(size)]))
    return pieces, me


def body(
    hidden_in,
    cached_out,
    cache_keys,
    cache_values,
    refresh_idx,
    modulation,
    q_gain,
    w_query,
    w_out,
    w_up,
    w_down,
):
    tokens, width = hidden_in.shape
    slots = refresh_idx.shape[0]
    uly_size = lax.axis_size("uly")
    blk_size = lax.axis_size("blk")
    local_heads = w_query.shape[1] // DH
    group = min(slots * uly_size, slots + (uly_size - 1) * OTHER)
    positions = lax.iota(jnp.int32, tokens)
    select = (positions[:, None] == refresh_idx[None, :]).astype(jnp.bfloat16)
    rows_in = jnp.einsum("ps,pd->sd", select, hidden_in, preferred_element_type=jnp.float32)
    norm_attn = layer_norm(rows_in, modulation[0], modulation[1]).astype(jnp.bfloat16)
    live_flag = jnp.broadcast_to((refresh_idx >= 0).astype(jnp.bfloat16)[:, None], (slots, DH))
    group_all = lax.all_gather(
        jnp.concatenate([norm_attn, live_flag], axis=1), "uly", axis=0, tiled=True
    )
    group_rows = group_all[:, :width]
    live = group_all[:, width].astype(jnp.float32)
    key_split = cache_keys.reshape(tokens, uly_size, local_heads, DH)
    value_split = cache_values.reshape(tokens, uly_size, local_heads, DH)
    key_rows = lax.all_to_all(key_split, "uly", split_axis=1, concat_axis=0, tiled=True)[:, 0]
    value_rows = lax.all_to_all(value_split, "uly", split_axis=1, concat_axis=0, tiled=True)[:, 0]

    everyone = slots * uly_size
    order = lax.iota(jnp.int32, everyone)
    before = (order[None, :] < order[:, None]).astype(jnp.float32)
    rank = jnp.sum(before * live[None, :], axis=1)
    compact = (
        (rank[None, :] == lax.iota(jnp.float32, group)[:, None]) & (live[None, :] > 0)
    ).astype(jnp.bfloat16)

    projected = jnp.dot(group_rows, w_query, preferred_element_type=jnp.float32).reshape(
        -1, local_heads, DH
    )
    squares = jnp.mean(projected * projected, axis=-1, keepdims=True)
    projected = projected * lax.rsqrt(squares + 1e-06) * (q_gain / math.sqrt(DH))
    projected = projected.astype(jnp.bfloat16).reshape(everyone, local_heads * DH)
    projected = jnp.dot(compact, projected, preferred_element_type=jnp.float32).astype(jnp.bfloat16)
    queries = lax.all_gather(
        projected.reshape(group, local_heads, DH), "blk", axis=0, tiled=True
    )
    scores = jnp.einsum("qhd,khd->hqk", queries, key_rows, preferred_element_type=jnp.float32)
    maxima = jnp.max(scores, axis=-1)
    weights = jnp.exp(scores - maxima[..., None])
    denominators = jnp.sum(weights, axis=-1)
    weighted = jnp.einsum(
        "hqk,khd->hqd", weights.astype(jnp.bfloat16), value_rows, preferred_element_type=jnp.float32
    )
    extra = jnp.concatenate(
        [
            jnp.broadcast_to(maxima[..., None], maxima.shape + (DH // 2,)),
            jnp.broadcast_to(denominators[..., None], maxima.shape + (DH // 2,)),
        ],
        axis=-1,
    )
    packed = jnp.concatenate([weighted, extra], axis=-1)
    packed = packed.reshape(local_heads, blk_size, group, 2 * DH).transpose(1, 0, 2, 3)
    packed = swap(packed, "blk")
    part_max = packed[..., DH]
    part_sum = packed[..., DH + DH // 2]
    top = jnp.max(part_max, axis=0)
    factor = jnp.exp(part_max - top[None])
    total = jnp.sum(part_sum * factor, axis=0)
    attended = jnp.sum(packed[..., :DH] * factor[..., None], axis=0) / total[..., None]
    attended = attended.astype(jnp.bfloat16).transpose(1, 0, 2).reshape(group, local_heads * DH)
    attended = jnp.dot(compact.T, attended, preferred_element_type=jnp.float32).astype(jnp.bfloat16)
    terms = jnp.dot(attended, w_out, preferred_element_type=jnp.float32)
    terms = swap(terms.reshape(uly_size, slots, width), "uly")
    branch = jnp.sum(terms, axis=0)
    after_attn = rows_in + modulation[2] * branch
    norm_mlp = layer_norm(after_attn, modulation[3], modulation[4]).astype(jnp.bfloat16)
    pieces, me = gather_permute(norm_mlp, "blk")
    lifted = jnp.dot(jnp.concatenate(pieces, axis=0), w_up, preferred_element_type=jnp.float32)
    activations = jax.nn.gelu(lifted, approximate=True).astype(jnp.bfloat16)
    down = jnp.dot(activations, w_down, preferred_element_type=jnp.float32).astype(jnp.bfloat16)
    down = down.reshape(blk_size, slots, width)
    total_down = down[0].astype(jnp.float32)
    for step in range(1, blk_size):
        back = lax.ppermute(
            down[step], "blk", [(i, (i - step) % blk_size) for i in range(blk_size)]
        )
        total_down = total_down + back.astype(jnp.float32)
    renewed = (after_attn + modulation[5] * total_down).astype(jnp.bfloat16)
    covered = jnp.sum(select.astype(jnp.float32), axis=1, keepdims=True)
    placed = jnp.dot(select, renewed, preferred_element_type=jnp.float32)
    blended = cached_out.astype(jnp.float32) * (1.0 - covered) + placed
    return blended.astype(jnp.bfloat16)


def solution(mesh):
    return jax.shard_map(
        body,
        mesh=mesh,
        in_specs=(
            P(("blk", "uly"), None),
            P(("blk", "uly"), None),
            P(("blk", "uly"), None),
            P(("blk", "uly"), None),
            P(("blk", "uly")),
            P(),
            P(),
            P(None, "uly"),
            P("uly", None),
            P(None, "blk"),
            P("blk", None),
        ),
        out_specs=P(("blk", "uly"), None),
        check_vma=False,
    )
```

time: 255 us -> 154 us (0.60)
  waiting for transfers between devices: 130 us -> 12.4 us
  blocking collectives: 62.3 us -> 82.6 us
  between operations: 13.3 us -> 0.41 us
  starting transfers between devices: 10.4 us -> 23.2 us
  matrix products: 25.9 us -> 18.8 us
    reduce_scatter x3 -> x0, waiting for transfers between devices: 98.1 us -> none  [the longest x1 41.3 us: body(): lax.psum_scatter(weighted, 'blk', scatter_dimension=0, tiled=True)]
    all_to_all x0 -> x2, blocking collectives: none -> 52.7 us  [swap(): return lax.all_to_all(parts, axis, split_axis=0, concat_axis=0, tiled=True)]
    unnamed x5 -> x0, waiting for transfers between devices: 31.9 us -> none
    pmax x1 -> x0, blocking collectives: 23.6 us -> none  [row_peak(): return lax.pmax(local_max, 'blk')]
    ppermute x0 -> x14, starting transfers between devices: none -> 13.2 us  [the longest x7 8.25 us: body(): lax.ppermute(down[step], 'blk', [(i, (i - step) % blk_size) for i in rang...]
    ppermute x0 -> x14, waiting for transfers between devices: none -> 12.4 us  [the longest x7 6.68 us: body(): lax.ppermute(down[step], 'blk', [(i, (i - step) % blk_size) for i in rang...]
    all_gather x3 -> x2, blocking collectives: 38.7 us -> 29.9 us  [the longest x1 19.9 us: body(): lax.all_gather(jnp.concatenate([norm_attn, live_flag], axis=1), 'uly', ax...]
    dot_general x4 -> x5, matrix products: 19.7 us -> 14 us  [the longest x1 9.3 us: body(): jnp.dot(activations, w_down, preferred_element_type=jnp.float32)]
  transfers between devices with their start and end apart: 6 -> 16, of which waited for: 4 -> 9; matrix products, arithmetic and copies ran while one was open for 5% -> 5% of each run, Pallas kernels for 0% -> 0%
where the time goes in v1:
time: 154 us; the launch traced here: 153 us
  blocking collectives  82.6 us (54%)
  starting transfers between devices  23.2 us (15%)
  matrix products  18.8 us (12%)
  waiting for transfers between devices  12.4 us (8%)
  local copies, waits for them, and re-layouts  9.03 us (6%)
  other arithmetic  6.91 us (4%)
    all_to_all x2, blocking collectives, swap(): return lax.all_to_all(parts, axis, split_axis=0, concat_axis=0, tiled=True)  52.7 us
    all_gather x1, blocking collectives, body(): lax.all_gather(jnp.concatenate([norm_attn, live_flag], axis=1), 'uly', ax...  19.9 us
    all_gather x1, blocking collectives, body(): lax.all_gather(projected.reshape(group, local_heads, DH), 'blk', axis=0,...  10 us
    dot_general x1, matrix products, body(): jnp.dot(activations, w_down, preferred_element_type=jnp.float32)  9.3 us
    ppermute x7, starting transfers between devices, body(): lax.ppermute(down[step], 'blk', [(i, (i - step) % blk_size) for i in rang...  8.25 us
    ppermute x7, waiting for transfers between devices, body(): lax.ppermute(down[step], 'blk', [(i, (i - step) % blk_size) for i in rang...  6.68 us
    all_to_all x1, starting transfers between devices, body(): lax.all_to_all(key_split, 'uly', split_axis=1, concat_axis=0, tiled=True)  6.32 us
    ppermute x7, waiting for transfers between devices, gather_permute(): lax.ppermute(rows, axis, [(i, (i + step) % size) for i in range(size)])  5.73 us
  transfers between devices with their start and end apart: 16, of which 9 were waited for; matrix products, arithmetic and copies ran while one was open for 5% of the time, Pallas kernels for 0%

profile of v1, /device:TPU:0, one launch (start us, length us, event | category | flops | bytes accessed | tf_op | source)
XLA Modules:
  0.0 153.3 jit_solution(13272242291857612285)
XLA Ops:
  0.0 1.5 %reshape.99 = bf16[64,4,6,128]{3,2,1,0:T(8,128)(2,1)S(1)} reshape(bf16[64,3072]{1,0:T(8,128)(2,1)} %param.13) | data formatting | bytes 786432 | tf_op jit(solution)/shard_map/reshape | solution.py:61
  2.5 6.3 %all-to-all-start = ((bf16[64,4,6,128]{3,0,2,1:T(8,128)(2,1)}), bf16[64,4,6,128]{3,0,2,1:T(8,128)(2,1)S(1)}, u32[]{:S(2)}, u32[]{:S(2)}) async-start(bf16[64,4,6,128]{3,0,2,1:T(8,128)(2,1)} %copy.58), calls=%async_computation | async-start | bytes 786432 | tf_op jit(solution)/shard_map/all_to_all | solution.py:63
  10.2 19.9 %all_gather.6 = bf16[64,3200]{1,0:T(8,128)(2,1)S(1)} all-gather(bf16[16,3200]{1,0:T(8,128)(2,1)S(1)} %pad_maximum_fusion.1), channel_id=1, replica_groups=mesh['blk'=8,'uly'=4] {'uly'}, dimensions={0}, use_global_device_ids=true | all-gather | bytes 512000 | tf_op jit(solution)/shard_map/all_gather | solution.py:56
  30.1 3.3 %fusion.61 = (f32[64,768]{1,0:T(8,128)S(1)}, f32[64,768]{1,0:T(8,128)S(1)}) fusion(bf16[3072,768]{1,0:T(8,128)(2,1)} %param.18, bf16[64,3200]{1,0:T(8,128)(2,1)S(1)} %all_gather.6), kind=kOutput, calls=%fused_computation.99 | convolution fusion | flops 302039040 | bytes 5505024 | tf_op jit(solution)/shard_map/dot_general | solution.py:74
  35.3 3.7 %all-to-all-start.1 = ((bf16[64,4,6,128]{3,0,2,1:T(8,128)(2,1)}), bf16[64,4,6,128]{3,0,2,1:T(8,128)(2,1)S(1)}, u32[]{:S(2)}, u32[]{:S(2)}) async-start(bf16[64,4,6,128]{3,0,2,1:T(8,128)(2,1)} %copy.60), calls=%async_computation.1 | async-start | bytes 786432 | tf_op jit(solution)/shard_map/all_to_all | solution.py:64
  39.5 10.0 %all_gather.7 = bf16[320,6,128]{2,0,1:T(8,128)(2,1)S(1)} all-gather(bf16[40,6,128]{2,0,1:T(8,128)(2,1)S(1)} %bitcast.82), channel_id=1, replica_groups=mesh['blk'=8,'uly'=4] {'blk'}, dimensions={0}, use_global_device_ids=true | all-gather | bytes 552960 | tf_op jit(solution)/shard_map/all_gather | solution.py:81
  52.5 27.8 %all_to_all.40 = f32[8,6,40,256]{3,2,1,0:T(8,128)S(1)} all-to-all(f32[8,6,40,256]{3,2,1,0:T(8,128)S(1)} %bitcast.75), channel_id=1, replica_groups=mesh['blk'=8,'uly'=4] {'blk'}, dimensions={0} | all-to-all | bytes 3932160 | tf_op jit(solution)/shard_map/all_to_all | solution.py:20
  80.3 1.3 slice_reduce_fusion
  81.6 2.2 %copy.70 = f32[8,6,40,1]{2,0,1,3:T(8,128)} copy(f32[8,6,40,1]{3,2,1,0:T(8,128)} %get-tuple-element.11) | data formatting | bytes 15360
  88.0 3.5 %fusion.3 = f32[64,3072]{1,0:T(8,128)S(1)} fusion(bf16[768,3072]{1,0:T(8,128)(2,1)} %param.19, f32[64]{0:T(128)} %copy-done.10, pred[64]{0:T(512)(128)(4,1)} %copy-done.9, f32[40,6]{0,1:T(8,128)S(1)} %bitcast.89, f32[6,40,128]{2,1,0:T(8,128)S(1)} %fusion.7), kind=kOutput, calls=%fused_computation.10 | convolution fusion | flops 306037760 | bytes 5629184 | tf_op jit(solution)/shard_map/dot_general | solution.py:109
  91.5 24.9 %all_to_all.41 = f32[4,16,3072]{2,1,0:T(8,128)S(1)} all-to-all(f32[4,16,3072]{2,1,0:T(8,128)S(1)} %bitcast.76), channel_id=1, replica_groups=mesh['blk'=8,'uly'=4] {'uly'}, dimensions={0} | all-to-all | bytes 1572864 | tf_op jit(solution)/shard_map/all_to_all | solution.py:20
  117.8 1.4 collective-permute-start.2
  119.2 1.4 collective-permute-start.3
  120.7 1.9 %collective-permute-done = bf16[16,3072]{1,0:T(8,128)(2,1)S(1)} collective-permute-done((bf16[16,3072]{1,0:T(8,128)(2,1)S(1)}, bf16[16,3072]{1,0:T(8,128)(2,1)S(1)}, u32[]{:S(2)}, u32[]{:S(2)}) %collective-permute-start) | collective-permute-done | bytes 98336 | tf_op jit(solution)/shard_map/ppermute | solution.py:28
  124.6 2.5 %collective-permute-done.2 = bf16[16,3072]{1,0:T(8,128)(2,1)S(1)} collective-permute-done((bf16[16,3072]{1,0:T(8,128)(2,1)S(1)}, bf16[16,3072]{1,0:T(8,128)(2,1)S(1)}, u32[]{:S(2)}, u32[]{:S(2)}) %collective-permute-start.2) | collective-permute-done | bytes 98336 | tf_op jit(solution)/shard_map/ppermute | solution.py:28
  127.8 9.3 %convolution_convert_fusion = bf16[128,3072]{1,0:T(8,128)(2,1)S(1)} fusion(bf16[1536,3072]{1,0:T(8,128)(2,1)} %param.21, bf16[128,3072]{1,0:T(8,128)(2,1)S(1)} %constant_dynamic-update-slice_fusion, bf16[3072,1536]{1,0:T(8,128)(2,1)} %param.20), kind=kOutput, calls=%fused_computation | convolution fusion | flops 2418081792 | bytes 20447232 | tf_op jit(solution)/shard_map/dot_general | solution.py:117
  137.1 1.3 collective-permute-start.10
  138.4 2.3 %collective-permute-start.11 = (bf16[16,3072]{1,0:T(8,128)(2,1)S(1)}, bf16[16,3072]{1,0:T(8,128)(2,1)S(1)}, u32[]{:S(2)}, u32[]{:S(2)}) collective-permute-start(bf16[16,3072]{1,0:T(8,128)(2,1)S(1)} %get-tuple-element.15), channel_id=1, source_target_pairs={{0,12},{4,16},{8,20},{12,24},{16,28},{20,0},{24,4},{28,8},{1,13},{... | collective-permute-start | bytes 294920 | tf_op jit(solution)/shard_map/ppermute | solution.py:121
  141.8 2.5 %collective-permute-start.7 = (bf16[16,3072]{1,0:T(8,128)(2,1)S(1)}, bf16[16,3072]{1,0:T(8,128)(2,1)S(1)}, u32[]{:S(2)}, u32[]{:S(2)}) collective-permute-start(bf16[16,3072]{1,0:T(8,128)(2,1)S(1)} %get-tuple-element.12), channel_id=1, source_target_pairs={{0,28},{4,0},{8,4},{12,8},{16,12},{20,16},{24,20},{28,24},{1,29},{... | collective-permute-start | bytes 294920 | tf_op jit(solution)/shard_map/ppermute | solution.py:121
  144.3 1.2 collective-permute-start.8
  145.5 2.7 %collective-permute-done.11 = bf16[16,3072]{1,0:T(8,128)(2,1)S(1)} collective-permute-done((bf16[16,3072]{1,0:T(8,128)(2,1)S(1)}, bf16[16,3072]{1,0:T(8,128)(2,1)S(1)}, u32[]{:S(2)}, u32[]{:S(2)}) %collective-permute-start.11) | collective-permute-done | bytes 98336 | tf_op jit(solution)/shard_map/ppermute | solution.py:121
  148.2 2.2 %collective-permute-done.8 = bf16[16,3072]{1,0:T(8,128)(2,1)S(1)} collective-permute-done((bf16[16,3072]{1,0:T(8,128)(2,1)S(1)}, bf16[16,3072]{1,0:T(8,128)(2,1)S(1)}, u32[]{:S(2)}, u32[]{:S(2)}) %collective-permute-start.8) | collective-permute-done | bytes 98336 | tf_op jit(solution)/shard_map/ppermute | solution.py:121
  150.3 1.8 %collective-permute-done.9 = bf16[16,3072]{1,0:T(8,128)(2,1)S(1)} collective-permute-done((bf16[16,3072]{1,0:T(8,128)(2,1)S(1)}, bf16[16,3072]{1,0:T(8,128)(2,1)S(1)}, u32[]{:S(2)}, u32[]{:S(2)}) %collective-permute-start.9) | collective-permute-done | bytes 98336 | tf_op jit(solution)/shard_map/ppermute | solution.py:121
  152.2 1.1 fusion
  (98 shorter events, 16.9 us)
Async XLA Ops:
  0.0 9.4 %copy-start.3 = (f32[6,3072]{1,0:T(8,128)S(1)}, f32[6,3072]{1,0:T(8,128)}, u32[]{:S(2)}) copy-start(f32[6,3072]{1,0:T(8,128)} %param.16) | copy-start | bytes 221188
  2.5 32.8 %all-to-all-start = ((bf16[64,4,6,128]{3,0,2,1:T(8,128)(2,1)}), bf16[64,4,6,128]{3,0,2,1:T(8,128)(2,1)S(1)}, u32[]{:S(2)}, u32[]{:S(2)}) async-start(bf16[64,4,6,128]{3,0,2,1:T(8,128)(2,1)} %copy.58), calls=%async_computation | async-start | bytes 786432 | tf_op jit(solution)/shard_map/all_to_all | solution.py:63
  35.2 14.9 %copy-start.9 = (pred[64]{0:T(512)(128)(4,1)}, pred[64]{0:T(512)(128)(4,1)S(1)}, u32[]{:S(2)}) copy-start(pred[64]{0:T(512)(128)(4,1)S(1)} %broadcast_compare_fusion) | copy-start | bytes 196
  35.3 14.3 %all-to-all-start.1 = ((bf16[64,4,6,128]{3,0,2,1:T(8,128)(2,1)}), bf16[64,4,6,128]{3,0,2,1:T(8,128)(2,1)S(1)}, u32[]{:S(2)}, u32[]{:S(2)}) async-start(bf16[64,4,6,128]{3,0,2,1:T(8,128)(2,1)} %copy.60), calls=%async_computation.1 | async-start | bytes 786432 | tf_op jit(solution)/shard_map/all_to_all | solution.py:64
  39.2 11.0 %copy-start.10 = (f32[64]{0:T(128)}, f32[64]{0:T(128)S(1)}, u32[]{:S(2)}) copy-start(f32[64]{0:T(128)S(1)} %select_reduce_fusion) | copy-start | bytes 772
  91.5 25.0 %copy-start.6 = (f32[1,3072]{1,0:T(1,128)S(1)}, f32[1,3072]{1,0:T(1,128)}, u32[]{:S(2)}) copy-start(f32[1,3072]{1,0:T(1,128)} %get-tuple-element.22) | copy-start | bytes 36868
  91.5 25.4 %copy-start.4 = (f32[1,3072]{1,0:T(1,128)S(1)}, f32[1,3072]{1,0:T(1,128)}, u32[]{:S(2)}) copy-start(f32[1,3072]{1,0:T(1,128)} %get-tuple-element.23) | copy-start | bytes 36868
  91.5 25.4 %copy-start.5 = (f32[1,3072]{1,0:T(1,128)S(1)}, f32[1,3072]{1,0:T(1,128)}, u32[]{:S(2)}) copy-start(f32[1,3072]{1,0:T(1,128)} %get-tuple-element.24) | copy-start | bytes 36868
  117.0 5.6 %collective-permute-start = (bf16[16,3072]{1,0:T(8,128)(2,1)S(1)}, bf16[16,3072]{1,0:T(8,128)(2,1)S(1)}, u32[]{:S(2)}, u32[]{:S(2)}) collective-permute-start(bf16[16,3072]{1,0:T(8,128)(2,1)S(1)} %get-tuple-element.6), channel_id=1, source_target_pairs={{0,4},{4,8},{8,12},{12,16},{16,20},{20,24},{24,28},{28,0},{1,5},{5... | collective-permute-start | bytes 294920 | tf_op jit(solution)/shard_map/ppermute | solution.py:28
  117.0 6.7 %collective-permute-start.1 = (bf16[16,3072]{1,0:T(8,128)(2,1)S(1)}, bf16[16,3072]{1,0:T(8,128)(2,1)S(1)}, u32[]{:S(2)}, u32[]{:S(2)}) collective-permute-start(bf16[16,3072]{1,0:T(8,128)(2,1)S(1)} %get-tuple-element.6), channel_id=1, source_target_pairs={{0,8},{4,12},{8,16},{12,20},{16,24},{20,28},{24,0},{28,4},{1,9},{5... | collective-permute-start | bytes 294920 | tf_op jit(solution)/shard_map/ppermute | solution.py:28
  117.8 9.4 %collective-permute-start.2 = (bf16[16,3072]{1,0:T(8,128)(2,1)S(1)}, bf16[16,3072]{1,0:T(8,128)(2,1)S(1)}, u32[]{:S(2)}, u32[]{:S(2)}) collective-permute-start(bf16[16,3072]{1,0:T(8,128)(2,1)S(1)} %get-tuple-element.6), channel_id=1, source_target_pairs={{0,12},{4,16},{8,20},{12,24},{16,28},{20,0},{24,4},{28,8},{1,13},{... | collective-permute-start | bytes 294920 | tf_op jit(solution)/shard_map/ppermute | solution.py:28
  119.2 8.1 %collective-permute-start.3 = (bf16[16,3072]{1,0:T(8,128)(2,1)S(1)}, bf16[16,3072]{1,0:T(8,128)(2,1)S(1)}, u32[]{:S(2)}, u32[]{:S(2)}) collective-permute-start(bf16[16,3072]{1,0:T(8,128)(2,1)S(1)} %get-tuple-element.6), channel_id=1, source_target_pairs={{0,16},{4,20},{8,24},{12,28},{16,0},{20,4},{24,8},{28,12},{1,17},{... | collective-permute-start | bytes 294920 | tf_op jit(solution)/shard_map/ppermute | solution.py:28
  120.7 6.8 %collective-permute-start.4 = (bf16[16,3072]{1,0:T(8,128)(2,1)S(1)}, bf16[16,3072]{1,0:T(8,128)(2,1)S(1)}, u32[]{:S(2)}, u32[]{:S(2)}) collective-permute-start(bf16[16,3072]{1,0:T(8,128)(2,1)S(1)} %get-tuple-element.6), channel_id=1, source_target_pairs={{0,20},{4,24},{8,28},{12,0},{16,4},{20,8},{24,12},{28,16},{1,21},{... | collective-permute-start | bytes 294920 | tf_op jit(solution)/shard_map/ppermute | solution.py:28
  122.5 5.2 %collective-permute-start.5 = (bf16[16,3072]{1,0:T(8,128)(2,1)S(1)}, bf16[16,3072]{1,0:T(8,128)(2,1)S(1)}, u32[]{:S(2)}, u32[]{:S(2)}) collective-permute-start(bf16[16,3072]{1,0:T(8,128)(2,1)S(1)} %get-tuple-element.6), channel_id=1, source_target_pairs={{0,24},{4,28},{8,0},{12,4},{16,8},{20,12},{24,16},{28,20},{1,25},{... | collective-permute-start | bytes 294920 | tf_op jit(solution)/shard_map/ppermute | solution.py:28
  123.7 4.0 %collective-permute-start.6 = (bf16[16,3072]{1,0:T(8,128)(2,1)S(1)}, bf16[16,3072]{1,0:T(8,128)(2,1)S(1)}, u32[]{:S(2)}, u32[]{:S(2)}) collective-permute-start(bf16[16,3072]{1,0:T(8,128)(2,1)S(1)} %get-tuple-element.6), channel_id=1, source_target_pairs={{0,28},{4,0},{8,4},{12,8},{16,12},{20,16},{24,20},{28,24},{1,29},{... | collective-permute-start | bytes 294920 | tf_op jit(solution)/shard_map/ppermute | solution.py:28
  127.7 12.9 %copy-start.8 = (s32[16]{0:T(128)S(1)}, s32[16]{0:T(128)}, u32[]{:S(2)}) copy-start(s32[16]{0:T(128)} %param.15) | copy-start | bytes 196
  127.8 24.4 %copy-start.2 = (bf16[64,3072]{1,0:T(8,128)(2,1)S(1)}, bf16[64,3072]{1,0:T(8,128)(2,1)}, u32[]{:S(2)}) copy-start(bf16[64,3072]{1,0:T(8,128)(2,1)} %param.12) | copy-start | bytes 1179652
  137.1 7.2 %collective-permute-start.10 = (bf16[16,3072]{1,0:T(8,128)(2,1)S(1)}, bf16[16,3072]{1,0:T(8,128)(2,1)S(1)}, u32[]{:S(2)}, u32[]{:S(2)}) collective-permute-start(bf16[16,3072]{1,0:T(8,128)(2,1)S(1)} %get-tuple-element.16), channel_id=1, source_target_pairs={{0,16},{4,20},{8,24},{12,28},{16,0},{20,4},{24,8},{28,12},{1,17},{... | collective-permute-start | bytes 294920 | tf_op jit(solution)/shard_map/ppermute | solution.py:121
  138.4 9.7 %collective-permute-start.11 = (bf16[16,3072]{1,0:T(8,128)(2,1)S(1)}, bf16[16,3072]{1,0:T(8,128)(2,1)S(1)}, u32[]{:S(2)}, u32[]{:S(2)}) collective-permute-start(bf16[16,3072]{1,0:T(8,128)(2,1)S(1)} %get-tuple-element.15), channel_id=1, source_target_pairs={{0,12},{4,16},{8,20},{12,24},{16,28},{20,0},{24,4},{28,8},{1,13},{... | collective-permute-start | bytes 294920 | tf_op jit(solution)/shard_map/ppermute | solution.py:121
  140.8 7.4 %collective-permute-start.12 = (bf16[16,3072]{1,0:T(8,128)(2,1)S(1)}, bf16[16,3072]{1,0:T(8,128)(2,1)S(1)}, u32[]{:S(2)}, u32[]{:S(2)}) collective-permute-start(bf16[16,3072]{1,0:T(8,128)(2,1)S(1)} %get-tuple-element.14), channel_id=1, source_target_pairs={{0,8},{4,12},{8,16},{12,20},{16,24},{20,28},{24,0},{28,4},{1,9},{5... | collective-permute-start | bytes 294920 | tf_op jit(solution)/shard_map/ppermute | solution.py:121
  141.6 6.5 %collective-permute-start.13 = (bf16[16,3072]{1,0:T(8,128)(2,1)S(1)}, bf16[16,3072]{1,0:T(8,128)(2,1)S(1)}, u32[]{:S(2)}, u32[]{:S(2)}) collective-permute-start(bf16[16,3072]{1,0:T(8,128)(2,1)S(1)} %get-tuple-element.13), channel_id=1, source_target_pairs={{0,4},{4,8},{8,12},{12,16},{16,20},{20,24},{24,28},{28,0},{1,5},{5... | collective-permute-start | bytes 294920 | tf_op jit(solution)/shard_map/ppermute | solution.py:121
  141.8 6.4 %collective-permute-start.7 = (bf16[16,3072]{1,0:T(8,128)(2,1)S(1)}, bf16[16,3072]{1,0:T(8,128)(2,1)S(1)}, u32[]{:S(2)}, u32[]{:S(2)}) collective-permute-start(bf16[16,3072]{1,0:T(8,128)(2,1)S(1)} %get-tuple-element.12), channel_id=1, source_target_pairs={{0,28},{4,0},{8,4},{12,8},{16,12},{20,16},{24,20},{28,24},{1,29},{... | collective-permute-start | bytes 294920 | tf_op jit(solution)/shard_map/ppermute | solution.py:121
  144.3 6.1 %collective-permute-start.8 = (bf16[16,3072]{1,0:T(8,128)(2,1)S(1)}, bf16[16,3072]{1,0:T(8,128)(2,1)S(1)}, u32[]{:S(2)}, u32[]{:S(2)}) collective-permute-start(bf16[16,3072]{1,0:T(8,128)(2,1)S(1)} %get-tuple-element.18), channel_id=1, source_target_pairs={{0,24},{4,28},{8,0},{12,4},{16,8},{20,12},{24,16},{28,20},{1,25},{... | collective-permute-start | bytes 294920 | tf_op jit(solution)/shard_map/ppermute | solution.py:121
  148.1 4.0 %collective-permute-start.9 = (bf16[16,3072]{1,0:T(8,128)(2,1)S(1)}, bf16[16,3072]{1,0:T(8,128)(2,1)S(1)}, u32[]{:S(2)}, u32[]{:S(2)}) collective-permute-start(bf16[16,3072]{1,0:T(8,128)(2,1)S(1)} %get-tuple-element.17), channel_id=1, source_target_pairs={{0,20},{4,24},{8,28},{12,0},{16,4},{20,8},{24,12},{28,16},{1,21},{... | collective-permute-start | bytes 294920 | tf_op jit(solution)/shard_map/ppermute | solution.py:121
  (4 other events, 26.7 us)
